TPU v7x, 512 devices: a whole 4x4x16 slice. The times are simulated.
512 devices in a mesh: dp: 32 (over y, x, core), tensor: 16 (over z).
Axes of the slice: x: 4, y: 4, z: 16, core: 2. Of those that a mesh axis runs over, the one named last changes fastest.
Arguments:
- grad_out: bfloat16 [32, 256, 3072], P('dp', 'tensor'), may hold values from -6 to 6
- hidden: bfloat16 [32, 256, 12288], P('dp', None, 'tensor'), may hold values from -6 to 6
- error: bfloat16 [32, 3072, 12288], P('dp', None, 'tensor'), may hold values from -96 to 96
- q_init: float32 [12288, 32], P('tensor'), may hold values from -6 to 6
Outputs:
- basis: float32 [3072, 32], P('tensor')
- q_new: float32 [12288, 32], P('tensor')
All inputs are finite; a program needn't handle non-finite values.
Results may differ from a plain program's by a relative error of at most 0.0003.
Values may be sent and summed in bfloat16 or wider, within the bound.
A program may use at most 64 MiB of HBM per device.

v0:
```python
import jax
import jax.numpy as jnp
from jax import lax
from jax.sharding import PartitionSpec as P


def body(grad_out, hidden, error, q_init):
    high = lax.Precision.HIGHEST
    grads = grad_out[0]
    acts = hidden[0]
    memory = error[0]
    grad_matrix = memory.astype(jnp.float32) + jnp.einsum(
        "td,tf->df",
        lax.all_gather(grads, "tensor", axis=0, tiled=True),
        acts,
        preferred_element_type=jnp.float32,
    )
    p_part = jnp.dot(grad_matrix, q_init, precision=high)
    p_total = lax.psum(p_part, ("dp", "tensor"))
    gram = jnp.dot(p_total.T, p_total, precision=high)
    lower = jnp.linalg.cholesky(gram)
    p_hat = lax.linalg.triangular_solve(
        lower, p_total, left_side=False, lower=True, transpose_a=True
    )
    count = p_hat.shape[0] // lax.axis_size("tensor")
    p_rows = lax.dynamic_slice_in_dim(p_hat, lax.axis_index("tensor") * count, count, 0)
    q_part = jnp.einsum("df,dr->fr", grad_matrix, p_hat, precision=high)
    q_new = lax.psum(q_part, "dp") / lax.axis_size("dp")
    basis = p_rows * jnp.sqrt(jnp.float32(p_hat.shape[0]))
    return (basis, q_new)


def solution(mesh):
    return jax.shard_map(
        body,
        mesh=mesh,
        in_specs=(
            P("dp", "tensor", None),
            P("dp", None, "tensor"),
            P("dp", None, "tensor"),
            P("tensor", None),
        ),
        out_specs=(P("tensor", None), P("tensor", None)),
        check_vma=False,
    )
```

profile of v0, /device:TPU:1, one launch (start us, length us, event | category | flops | bytes accessed | tf_op | source)
XLA Modules:
  0.0 721.3 jit_solution(9661595932358660067)
XLA Ops:
  7.2 0.0 copy-start
  7.2 0.0 copy-start.3
  7.2 0.0 all-gather.3.cloned.1.call-start
  7.2 0.7 all-gather.3.cloned.1.call-update
  7.9 0.0 all-reduce.3.cloned.1.call-start
  8.0 70.1 %all-gather.3.cloned.1.call-done = bf16[1,256,3072]{2,1,0:T(8,128)(2,1)} async-done(((bf16[1,16,3072]{2,1,0:T(8,128)(2,1)}), bf16[1,256,3072]{2,1,0:T(8,128)(2,1)}) %all-gather.3.cloned.1.call-update) | async-done | bytes 1572880 | tf_op jit(solution)/shard_map/all_gather | solution.py:14
  78.1 0.0 copy-done
  78.1 0.0 copy-start.2
  78.1 3.0 fusion.4
  81.1 0.0 copy-start.1
  81.1 3.6 copy-done.1
  84.7 0.0 copy-done.3
  84.7 0.0 copy-done.2
  84.7 9.7 %fusion.1 = f32[3072,32]{0,1:T(8,128)} fusion(f32[768,32]{0,1:T(8,128)S(1)} %copy-done.3, f32[3072,768]{1,0:T(8,128)S(1)} %fusion.4, bf16[1,3072,768]{2,1,0:T(8,128)(2,1)S(1)} %copy-done.2), kind=kOutput, calls=%fused_computation.2 | convolution fusion | flops 910688256 | bytes 14647296 | tf_op jit(solution)/shard_map/dot_general | solution.py:18
  94.4 0.0 all-reduce.3.cloned.1.call-update
  94.4 0.2 all-reduce.5.cloned.1.call-start
  94.6 470.7 %all-reduce.3.cloned.1.call-done = f32[3072,32]{0,1:T(8,128)} async-done(((f32[3072,32]{0,1:T(8,128)}), f32[3072,32]{0,1:T(8,128)}) %all-reduce.3.cloned.1.call-update) | async-done | bytes 393232 | tf_op jit(solution)/shard_map/psum | solution.py:19
  565.3 1.6 fusion.11
  566.9 0.1 copy.6
  566.9 2.9 cholesky.16
  569.9 0.6 compare_reduce_fusion
  570.5 0.7 fusion.7
  571.2 2.4 custom-call.6
  573.6 1.5 fusion.8
  575.2 9.9 %fusion = f32[768,32]{0,1:T(8,128)} fusion(f32[3072,32]{0,1:T(8,128)S(1)} %fusion.8, f32[3072,768]{1,0:T(8,128)} %copy-done.1, bf16[1,3072,768]{2,1,0:T(8,128)(2,1)} %param.6), kind=kOutput, calls=%fused_computation.1 | convolution fusion | flops 910688256 | bytes 14647296 | tf_op jit(solution)/shard_map/df,dr->fr/dot_general | solution.py:27
  585.1 0.0 all-reduce.5.cloned.1.call-update
  585.1 0.7 dynamic-slice_multiply_fusion
  585.8 127.4 %all-reduce.5.cloned.1.call-done = f32[768,32]{0,1:T(8,128)} async-done(((f32[768,32]{0,1:T(8,128)}), f32[768,32]{0,1:T(8,128)}) %all-reduce.5.cloned.1.call-update) | async-done | bytes 98320 | tf_op jit(solution)/shard_map/psum | solution.py:28
  713.3 1.5 broadcast_multiply_fusion
  (2 shorter events, 0.0 us)
Async XLA Ops:
  7.2 70.9 %copy-start = (bf16[1,256,768]{2,1,0:T(8,128)(2,1)S(1)}, bf16[1,256,768]{2,1,0:T(8,128)(2,1)}, u32[]{:S(2)}) copy-start(bf16[1,256,768]{2,1,0:T(8,128)(2,1)} %param.5) | copy-start | bytes 1179652
  7.2 77.5 %copy-start.3 = (f32[768,32]{0,1:T(8,128)S(1)}, f32[768,32]{0,1:T(8,128)}, u32[]{:S(2)}) copy-start(f32[768,32]{0,1:T(8,128)} %param.7) | copy-start | bytes 294916
  7.2 70.9 %all-gather.3.cloned.1.call-start = ((), (), s32[]{:S(2)}) async-start(), calls=%async_computation.2 | async-start | bytes 1671168 | tf_op jit(solution)/shard_map/all_gather | solution.py:14
  7.9 557.4 %all-reduce.3.cloned.1.call-start = ((), (), s32[]{:S(2)}) async-start(), calls=%async_computation | async-start | bytes 786432 | tf_op jit(solution)/shard_map/psum | solution.py:19
  78.1 6.6 copy-start.2
  81.1 3.6 copy-start.1
  94.4 618.9 %all-reduce.5.cloned.1.call-start = ((), (), s32[]{:S(2)}) async-start(), calls=%async_computation.1 | async-start | bytes 196608 | tf_op jit(solution)/shard_map/psum | solution.py:28
Sparse Core Ops, SparseCore 0:
  10.1 67.9 all-gather.2
  94.5 470.7 all-reduce.2
  585.2 127.9 all-reduce.4
where the time goes:
time: 722 us; the launch traced here: 721 us
  waiting for transfers between devices  669 us (93%)
  matrix products  25.7 us (4%)
  between operations  13.8 us (2%)
  other arithmetic  8.93 us (1%)
    psum x1, waiting for transfers between devices, body(): p_total = lax.psum(p_part, ('dp', 'tensor'))  471 us
    psum x1, waiting for transfers between devices, body(): q_new = lax.psum(q_part, 'dp') / lax.axis_size('dp')  127 us
    all_gather x1, waiting for transfers between devices, body(): lax.all_gather(grads, 'tensor', axis=0, tiled=True)  70.1 us
  transfers between devices with their start and end apart: 3, of which 3 were waited for; matrix products, arithmetic and copies ran while one was open for 0% of the time, Pallas kernels for 0%

commit v1 on v0

v1 whole, which is shorter than its diff:
```python
import functools

import jax
import jax.numpy as jnp
from jax import lax
from jax.experimental import pallas as pl
from jax.experimental.pallas import tpu as pltpu
from jax.sharding import PartitionSpec as P

MESH = pl.DeviceIdType.MESH
NT = (((1,), (1,)), ((), ()))
NN = (((1,), (0,)), ((), ()))
F32, BF16 = jnp.float32, jnp.bfloat16
HIGH = lax.Precision.HIGHEST

NZ, CHIPS, DP = 16, 16, 32
D, F, R, TOK = 3072, 768, 32, 256
LANES, HALF, QUART = 128, 384, 768
SCALE = 2.0**20
OWNERS = [(4 * y + x) * 2 + c for y in range(4) for x in range(4) if x != y for c in range(2)]
TILES = len(OWNERS)


def dot(a, b, dims):
    return lax.dot_general(a, b, dims, preferred_element_type=F32)


def split(v):
    hi = v.astype(BF16)
    return hi, (v - hi.astype(F32)).astype(BF16)


def take(ref, sem):
    pltpu.make_async_copy(ref, ref, sem).wait()


def aligned(i, n):
    return pl.multiple_of(i, n)


def inverse_factor(gram):
    row = lax.broadcasted_iota(jnp.int32, (R, 2 * R), 0)
    col = lax.broadcasted_iota(jnp.int32, (R, 2 * R), 1)
    one = (col - R == row).astype(F32)
    a = jnp.concatenate([gram, one[:, R:]], axis=1)
    for k in range(R):
        pivot = a[k : k + 1, :]
        step = jnp.where(row[:, :1] > k, a[:, k : k + 1] / a[k : k + 1, k : k + 1], 0.0)
        a = a - step * pivot
    diag = jnp.sum(jnp.where(row == col, a, 0.0), axis=1, keepdims=True)
    return a[:, R:] / jnp.sqrt(diag)


def kernel(
    grad_hbm, hid_hbm, err_hbm, qt_hbm, basis_ref, qnew_ref,
    grad, hid, err, qt, hidp, pt, img_send, img_recv, core_recv, rs_send, rs_recv,
    red, zrecv, ptf, wrecv, s_send, s_recv, fin, linv,
    loc, img_s, img_r, core_s, core_r, rs_s, rs_r, zrs_s, zrs_r, zag_s, zag_r,
    ag_s, ag_r, fwd_s, fwd_r, w_s, w_r, srs_s, srs_r, sag_s, sag_r,
):
    dp = lax.axis_index("dp")
    z = lax.axis_index("tensor")
    core, chip = dp % 2, dp // 2
    x, y = chip % 4, chip // 4
    sibling = dp + 1 - 2 * core

    def send(src, dst, s, r, to):
        copy = pltpu.make_async_remote_copy(
            src_ref=src, dst_ref=dst, send_sem=s, recv_sem=r,
            device_id=to, device_id_type=MESH,
        )
        copy.start()

    loads = [
        pltpu.make_async_copy(qt_hbm, qt, loc.at[0]),
        pltpu.make_async_copy(hid_hbm, hid, loc.at[1]),
    ]
    loads += [
        pltpu.make_async_copy(
            err_hbm.at[pl.ds(c * QUART, QUART)], err.at[pl.ds(c * QUART, QUART)], loc.at[3 + c]
        )
        for c in range(4)
    ]
    loads.insert(2, pltpu.make_async_copy(grad_hbm, grad, loc.at[2]))
    for load in loads:
        load.start()

    barrier = pltpu.get_barrier_semaphore()
    for d in range(1, DP):
        pl.semaphore_signal(barrier, 1, device_id=((dp + d) % DP, z), device_id_type=MESH)
    for d in range(1, NZ):
        pl.semaphore_signal(barrier, 1, device_id=(dp, (z + d) % NZ), device_id_type=MESH)

    lane = lax.broadcasted_iota(jnp.int32, (8, LANES), 1)
    sends = []

    def finish():
        for fn in sends:
            fn()


    loads[0].wait()
    q_hi, q_lo = split(qt[...])
    q2 = jnp.concatenate([q_hi, q_lo], axis=0)
    loads[1].wait()
    images = dot(hid[...], jnp.concatenate([q2, q2], axis=0), NT).reshape(NZ, 2, 8, LANES)
    img_send[...] = jnp.where((lane < 2 * R)[None], images[:, 0], images[:, 1])
    loads[2].wait()
    pl.semaphore_wait(barrier, DP + NZ - 2)
    for d in range(1, NZ):
        to = (z + d) % NZ
        send(img_send.at[to], img_recv.at[d - 1], img_s, img_r, (dp, to))
    sends.append(lambda: take(img_send.at[pl.ds(0, NZ - 1)], img_s))

    for c in range(4):
        loads[3 + c].wait()
        part = dot(q2, err[pl.ds(c * QUART, QUART), :], NT)
        pt[:, pl.ds(c * QUART, QUART)] = part[:R] + part[R:]
    by_tile = hid[...].astype(F32).reshape(NZ, 2, 8, F)
    hidp[...] = jnp.concatenate([by_tile[:, 0], by_tile[:, 1]], axis=0).reshape(TOK, F).astype(BF16)

    take(img_recv, img_r)
    own = jnp.sum(img_recv[...], axis=0) + img_send[z]
    own = own.T
    own = jnp.concatenate([own[:R] + own[R : 2 * R], own[2 * R : 3 * R] + own[3 * R :]], axis=1)
    im_hi, im_lo = split(own)
    im2 = jnp.concatenate([im_hi, im_lo], axis=0)
    for c in range(4):
        cols = pl.ds(c * QUART, QUART)
        part = dot(im2, grad[:, cols], NN)
        pt[:, cols] += part[:R] + part[R:]
        theirs = pl.ds(aligned(c * QUART + (1 - core) * HALF, LANES), HALF)
        send(pt.at[:, theirs], core_recv.at[c], core_s, core_r.at[c], (sibling, z))
    sends.append(lambda: take(core_recv, core_s))

    for c in range(4):
        take(core_recv.at[c], core_r.at[c])
        mine = pt[:, pl.ds(aligned(c * QUART + core * HALF, LANES), HALF)] + core_recv[c]
        for g in range(4):
            t = 4 * c + g
            rs_send[t] = mine[8 * g : 8 * g + 8]

            @pl.when(t != chip)
            def _(t=t):
                send(rs_send.at[t], rs_recv.at[chip], rs_s, rs_r, (2 * t + core, z))

    sends.append(lambda: take(rs_send.at[pl.ds(0, CHIPS - 1)], rs_s))
    rs_recv[chip] = rs_send[chip]
    take(rs_recv.at[pl.ds(0, CHIPS - 1)], rs_r)
    red[...] = jnp.sum(rs_recv[...], axis=0)

    rows = pl.ds(aligned(8 * x, 8), 8)
    base = y * QUART + core * HALF
    place = [5 * t + 8 * core for t in range(3)]
    place = [lax.rem(p, NZ) for p in place]
    tile_at = [ptf.at[rows, pl.ds(aligned(base + t * LANES, LANES), LANES)] for t in range(3)]
    for t in range(3):

        @pl.when(z != place[t])
        def _(t=t):
            send(red.at[:, pl.ds(t * LANES, LANES)], zrecv.at[z], zrs_s, zrs_r, (dp, place[t]))

    for t in range(3):

        @pl.when(z == place[t])
        def _(t=t):
            zrecv[z] = red[:, t * LANES : (t + 1) * LANES]
            take(zrecv.at[pl.ds(0, NZ - 1)], zrs_r)
            tile_at[t][...] = jnp.sum(zrecv[...], axis=0) * SCALE
            for d in range(1, NZ):
                send(tile_at[t], tile_at[t], zag_s, zag_r.at[t], (dp, (z + d) % NZ))

    for t in range(3):

        @pl.when(z != place[t])
        def _(t=t):
            take(tile_at[t], zag_r.at[t])

    def z_sends():
        for t in range(3):

            @pl.when(z == place[t])
            def _():
                take(red.at[:, pl.ds(0, 2 * LANES)], zrs_s)
                take(zrecv.at[pl.ds(0, NZ - 1)], zag_s)

        @pl.when((z != place[0]) & (z != place[1]) & (z != place[2]))
        def _():
            take(red, zrs_s)

    sends.append(z_sends)

    window = ptf.at[rows, pl.ds(aligned(base, LANES), HALF)]
    for d in range(1, CHIPS):
        send(window, window, ag_s, ag_r.at[chip], (2 * ((chip + d) % CHIPS) + core, z))
    sends.append(lambda: take(rs_send.at[pl.ds(0, CHIPS - 1)], ag_s))
    for dy in range(4):
        yy = (y + dy) % 4
        for dx in range(1 if dy == 0 else 0, 4):
            xx = (x + dx) % 4
            there = ptf.at[
                pl.ds(aligned(8 * xx, 8), 8), pl.ds(aligned(yy * QUART + core * HALF, LANES), HALF)
            ]
            take(there, ag_r.at[4 * yy + xx])
        block = ptf.at[:, pl.ds(aligned(yy * QUART + core * HALF, LANES), HALF)]
        send(block, block, fwd_s, fwd_r, (sibling, z))
    sends.append(lambda: take(core_recv, fwd_s))
    take(core_recv, fwd_r)

    p_hi, p_lo = split(ptf[...])
    p2 = jnp.concatenate([p_hi, p_lo], axis=0)
    w = dot(grad[...], jnp.concatenate([p2, p2], axis=0), NT)
    wrecv[z] = jnp.where(lane < 2 * R, w[:8], w[8:])
    for d in range(1, NZ):
        send(wrecv.at[z], wrecv.at[z], w_s, w_r, (dp, (z + d) % NZ))
    sends.append(lambda: take(wrecv.at[pl.ds(0, NZ - 1)], w_s))

    part = dot(p2, err[...], NN)
    s_err = part[:R] + part[R:]
    gram = dot(p2, p2, NT)
    gram = gram[:R, :R] + gram[R:, R:] + (gram[:R, R:] + gram[R:, :R])

    take(wrecv.at[pl.ds(0, NZ - 1)], w_r)
    wt = wrecv[...].reshape(LANES, LANES).T
    wt = jnp.concatenate([wt[:R] + wt[R : 2 * R], wt[2 * R : 3 * R] + wt[3 * R :]], axis=1)
    w_hi, w_lo = split(wt)
    part = dot(jnp.concatenate([w_hi, w_lo], axis=0), hidp[...], NN)
    s = s_err + part[:R] + part[R:]

    for t, owner in enumerate(OWNERS):
        g, k = t // 6, t % 6
        s_send[t] = s[8 * g : 8 * g + 8, k * LANES : (k + 1) * LANES]

        @pl.when(dp != owner)
        def _(t=t, owner=owner):
            send(s_send.at[t], s_recv.at[dp], srs_s, srs_r, (owner, z))

    linv[...] = inverse_factor(gram)
    first = aligned((3 * z) // 2 * LANES, LANES)
    near = ptf[:, pl.ds(first, 2 * LANES)]
    near = jnp.where(z % 2 == 1, near[:, 64:], near[:, :192])
    basis_ref[...] = jnp.dot(linv[...], near, precision=HIGH, preferred_element_type=F32) * (
        float(D) ** 0.5
    )

    is_owner = x != y
    tile = (3 * y + x - (x > y).astype(jnp.int32)) * 2 + core
    g, k = tile // 6, tile % 6
    here = fin.at[pl.ds(aligned(8 * g, 8), 8), pl.ds(aligned(k * LANES, LANES), LANES)]

    @pl.when(is_owner)
    def _():
        s_recv[dp] = s_send[tile]
        take(s_recv.at[pl.ds(0, DP - 1)], srs_r)
        here[...] = jnp.sum(s_recv[...], axis=0)
        for d in range(1, DP):
            send(here, here, sag_s, sag_r, ((dp + d) % DP, z))
        take(s_send.at[pl.ds(0, TILES - 1)], sag_r)

    @pl.when(jnp.logical_not(is_owner))
    def _():
        take(s_send, sag_r)

    def s_sends():
        @pl.when(is_owner)
        def _():
            take(s_send.at[pl.ds(0, TILES - 1)], srs_s)
            take(s_recv.at[pl.ds(0, DP - 1)], sag_s)

        @pl.when(jnp.logical_not(is_owner))
        def _():
            take(s_send, srs_s)

    sends.append(s_sends)
    qnew_ref[...] = jnp.dot(linv[...], fin[...], precision=HIGH, preferred_element_type=F32) * (
        1.0 / DP
    )
    finish()


def body(grad_out, hidden, error, q_init):
    one, many = pltpu.SemaphoreType.DMA, lambda n: pltpu.SemaphoreType.DMA((n,))
    vmem = pltpu.VMEM
    basis, q_new = pl.pallas_call(
        kernel,
        out_shape=(
            jax.ShapeDtypeStruct((R, D // NZ), F32),
            jax.ShapeDtypeStruct((R, F), F32),
        ),
        in_specs=[pl.BlockSpec(memory_space=pltpu.HBM)] * 4,
        out_specs=[pl.BlockSpec(memory_space=pltpu.VMEM)] * 2,
        scratch_shapes=[
            vmem((TOK // NZ, D), BF16),
            vmem((TOK, F), BF16),
            vmem((D, F), BF16),
            vmem((R, F), F32),
            vmem((TOK, F), BF16),
            vmem((R, D), F32),
            vmem((NZ, 8, LANES), F32),
            vmem((NZ - 1, 8, LANES), F32),
            vmem((4, R, HALF), F32),
            vmem((CHIPS, 8, HALF), F32),
            vmem((CHIPS, 8, HALF), F32),
            vmem((8, HALF), F32),
            vmem((NZ, 8, LANES), F32),
            vmem((R, D), F32),
            vmem((NZ, 8, LANES), F32),
            vmem((TILES, 8, LANES), F32),
            vmem((DP, 8, LANES), F32),
            vmem((R, F), F32),
            vmem((R, R), F32),
            many(7),
            one, one,
            one, many(4),
            one, one,
            one, one,
            one, many(3),
            one, many(CHIPS),
            one, one,
            one, one,
            one, one,
            one, one,
        ],
        compiler_params=pltpu.CompilerParams(
            collective_id=0, has_side_effects=True, vmem_limit_bytes=60 * 1024 * 1024
        ),
    )(grad_out[0], hidden[0], error[0], q_init.T)
    return basis.T, q_new.T


def solution(mesh):
    return jax.shard_map(
        body,
        mesh=mesh,
        in_specs=(
            P("dp", "tensor", None),
            P("dp", None, "tensor"),
            P("dp", None, "tensor"),
            P("tensor", None),
        ),
        out_specs=(P("tensor", None), P("tensor", None)),
        check_vma=False,
    )
```

time: 722 us -> 79.6 us (0.11)
  waiting for transfers between devices: 669 us -> 0 us
  Pallas kernels: 0 us -> 75.8 us
  matrix products: 25.7 us -> 0 us
  between operations: 13.8 us -> 0.64 us
  other arithmetic: 8.93 us -> 0 us
    psum x2 -> x0, waiting for transfers between devices: 598 us -> none  [the longest x1 471 us: body(): p_total = lax.psum(p_part, ('dp', 'tensor'))]
    pallas_call x0 -> x1, Pallas kernels: none -> 75.8 us  [body(): pl.pallas_call(kernel, out_shape=(jax.ShapeDtypeStruct((R, D // NZ), F32)...]
    all_gather x1 -> x0, waiting for transfers between devices: 70.1 us -> none  [body(): lax.all_gather(grads, 'tensor', axis=0, tiled=True)]
    dot_general x4 -> x0, matrix products: 24.2 us -> none  [the longest x1 9.93 us: body(): q_part = jnp.einsum('df,dr->fr', grad_matrix, p_hat, precision=high)]
  transfers between devices with their start and end apart: 3 -> 0, of which waited for: 3 -> 0; matrix products, arithmetic and copies ran while one was open for 0% -> 0% of each run, Pallas kernels for 0% -> 0%
where the time goes in v1:
time: 79.6 us; the launch traced here: 79.4 us
  Pallas kernels  75.8 us (95%)
  local copies, waits for them, and re-layouts  2.91 us (4%)
    pallas_call x1, Pallas kernels, body(): pl.pallas_call(kernel, out_shape=(jax.ShapeDtypeStruct((R, D // NZ), F32)...  75.8 us
    unnamed x2, local copies, waits for them, and re-layouts  2.91 us

profile of v1, /device:TPU:1, one launch (start us, length us, event | category | flops | bytes accessed | tf_op | source)
XLA Modules:
  0.0 79.4 jit_solution(13765269500433942585)
XLA Ops:
  0.6 75.8 %shard_map.59 = (f32[32,192]{1,0:T(8,128)}, f32[32,768]{1,0:T(8,128)}) custom-call(bf16[16,3072]{1,0:T(8,128)(2,1)} %bitcast.9, bf16[256,768]{1,0:T(8,128)(2,1)} %bitcast.7, bf16[3072,768]{1,0:T(8,128)(2,1)} %bitcast.6, f32[32,768]{1,0:T(8,128)} %bitcast.10), custom_call_target="tpu_custom_call" | custom-call | tf_op jit(solution)/shard_map/pallas_call | solution.py:284
  76.5 1.4 %copy.8 = f32[192,32]{0,1:T(8,128)} copy(f32[192,32]{0,1:T(8,128)} %bitcast.11) | data formatting | bytes 49152
  77.8 1.5 %copy.9 = f32[768,32]{0,1:T(8,128)} copy(f32[768,32]{0,1:T(8,128)} %bitcast.8) | data formatting | bytes 196608

commit v2 on v1

v2 whole, which is shorter than its diff:
```python
import functools

import jax
import jax.numpy as jnp
from jax import lax
from jax.experimental import pallas as pl
from jax.experimental.pallas import tpu as pltpu
from jax.sharding import PartitionSpec as P

MESH = pl.DeviceIdType.MESH
NT = (((1,), (1,)), ((), ()))
NN = (((1,), (0,)), ((), ()))
F32, BF16 = jnp.float32, jnp.bfloat16
HIGH = lax.Precision.HIGHEST

NZ, CHIPS, DP = 16, 16, 32
D, F, R, TOK = 3072, 768, 32, 256
LANES, HALF, QUART = 128, 384, 768
FAR_Z = sorted(range(1, NZ), key=lambda d: -min(d, NZ - d))
FAR_XY = sorted(range(1, CHIPS), key=lambda d: -min(d % 4, 4 - d % 4) - min(d // 4, 4 - d // 4))
SCALE = 2.0**20
BLOCK = TOK // NZ


def dot(a, b, dims):
    return lax.dot_general(a, b, dims, preferred_element_type=F32)


def split(v):
    hi = v.astype(BF16)
    return hi, (v - hi.astype(F32)).astype(BF16)


def take(ref, sem):
    pltpu.make_async_copy(ref, ref, sem).wait()


def aligned(i, n):
    return pl.multiple_of(i, n)


def sum_terms(v):
    return v + pltpu.roll(v, R, 1)


def pack(v):
    quarter = lax.broadcasted_iota(jnp.int32, (1, LANES), 1) // R
    v = jnp.where(quarter < 2, v[..., :8, :], v[..., 8:, :])
    return jnp.where(quarter % 2 == 0, v[..., :4, :], v[..., 4:, :])


def unpack(v):
    v = v.T
    return jnp.concatenate([v[R * g : R * g + R] for g in range(4)], axis=1)


def inverse_factor(gram):
    row = lax.broadcasted_iota(jnp.int32, (R, 2 * R), 0)
    col = lax.broadcasted_iota(jnp.int32, (R, 2 * R), 1)
    one = (col - R == row).astype(F32)
    a = jnp.concatenate([gram, one[:, R:]], axis=1)
    for k in range(R):
        pivot = a[k : k + 1, :]
        step = jnp.where(row[:, :1] > k, a[:, k : k + 1] / a[k : k + 1, k : k + 1], 0.0)
        a = a - step * pivot
    diag = jnp.sum(jnp.where(row == col, a, 0.0), axis=1, keepdims=True)
    return a[:, R:] / jnp.sqrt(diag)


def kernel(
    grad_hbm, hid_hbm, err_hbm, qt_hbm, basis_ref, qnew_ref,
    grad, hid, err, qt, hidp, pt, img_send, img_recv, core_recv, rs_send, rs_recv,
    red, znext, zrecv, ptf, wrecv, s_buf, s_core, sx, sy, sx2, sy2, linv,
    loc, img_s, img_r, core_s, core_r, rs_s, rs_r, zn_s, zn_r, z_s, z_r,
    ag_s, ag_r, fwd_s, fwd_r, w_s, w_r, sc_s, sc_r, sx_s, sx_r, sy_s, sy_r,
    sx2_s, sx2_r, sy2_s, sy2_r, q_s, q_r,
):
    dp = lax.axis_index("dp")
    z = lax.axis_index("tensor")
    core, chip = dp % 2, dp // 2
    x, y = chip % 4, chip // 4
    sibling = dp + 1 - 2 * core

    def chip_at(d):
        return 2 * (4 * ((y + d // 4) % 4) + (x + d % 4) % 4) + core

    def send(src, dst, s, r, to):
        copy = pltpu.make_async_remote_copy(
            src_ref=src, dst_ref=dst, send_sem=s, recv_sem=r,
            device_id=to, device_id_type=MESH,
        )
        copy.start()

    loads = [
        pltpu.make_async_copy(qt_hbm, qt, loc.at[0]),
        pltpu.make_async_copy(hid_hbm, hid, loc.at[1]),
    ]
    loads += [
        pltpu.make_async_copy(
            err_hbm.at[pl.ds(c * QUART, QUART)], err.at[pl.ds(c * QUART, QUART)], loc.at[3 + c]
        )
        for c in range(4)
    ]
    loads.insert(2, pltpu.make_async_copy(grad_hbm, grad, loc.at[2]))
    for load in loads:
        load.start()

    barrier = pltpu.get_barrier_semaphore()
    pl.semaphore_signal(barrier, 1, device_id=(sibling, z), device_id_type=MESH)
    for d in FAR_XY:
        to = chip_at(d)
        pl.semaphore_signal(barrier, 1, device_id=(to, z), device_id_type=MESH)
    for d in FAR_Z:
        pl.semaphore_signal(barrier, 1, device_id=(dp, (z + d) % NZ), device_id_type=MESH)

    sends = []

    def finish():
        for fn in sends:
            fn()


    loads[0].wait()
    q_hi, q_lo = split(qt[...])
    q2 = jnp.concatenate([q_hi, q_lo], axis=0)
    loads[1].wait()
    images = sum_terms(dot(hid[...], jnp.concatenate([q2, q2], axis=0), NT))
    img_send[...] = pack(images.reshape(NZ, BLOCK, LANES))
    loads[2].wait()
    pl.semaphore_wait(barrier, CHIPS + NZ - 1)
    for d in FAR_Z:
        to = (z + d) % NZ
        send(img_send.at[to], img_recv.at[d - 1], img_s, img_r, (dp, to))
    sends.append(lambda: take(img_send.at[pl.ds(0, NZ - 1)], img_s))

    for c in range(4):
        loads[3 + c].wait()
        part = dot(q2, err[pl.ds(c * QUART, QUART), :], NT)
        pt[:, pl.ds(c * QUART, QUART)] = part[:R] + part[R:]
    by_quarter = hid[...].astype(F32).reshape(NZ, 4, 4, F)
    by_quarter = [by_quarter[:, g].reshape(TOK // 4, F) for g in range(4)]
    hidp[...] = jnp.concatenate(by_quarter, axis=0).astype(BF16)

    take(img_recv, img_r)
    im_hi, im_lo = split(unpack(jnp.sum(img_recv[...], axis=0) + img_send[z]))
    im2 = jnp.concatenate([im_hi, im_lo], axis=0)
    for c in range(4):
        cols = pl.ds(c * QUART, QUART)
        part = dot(im2, grad[:, cols], NN)
        pt[:, cols] += part[:R] + part[R:]
        theirs = pl.ds(aligned(c * QUART + (1 - core) * HALF, LANES), HALF)
        send(pt.at[:, theirs], core_recv.at[c], core_s, core_r.at[c], (sibling, z))
    sends.append(lambda: take(core_recv, core_s))

    for c in range(4):
        take(core_recv.at[c], core_r.at[c])
        mine = pt[:, pl.ds(aligned(c * QUART + core * HALF, LANES), HALF)] + core_recv[c]
        for g in range(4):
            t = 4 * c + g
            rs_send[t] = mine[8 * g : 8 * g + 8]

            @pl.when(t != chip)
            def _(t=t):
                send(rs_send.at[t], rs_recv.at[chip], rs_s, rs_r, (2 * t + core, z))

    sends.append(lambda: take(rs_send.at[pl.ds(0, CHIPS - 1)], rs_s))
    rs_recv[chip] = rs_send[chip]
    take(rs_recv.at[pl.ds(0, CHIPS - 1)], rs_r)
    red[...] = jnp.sum(rs_recv[...], axis=0)

    rows = pl.ds(aligned(8 * x, 8), 8)
    base = y * QUART + core * HALF
    window = ptf.at[rows, pl.ds(aligned(base, LANES), HALF)]
    send(red, znext, zn_s, zn_r, (dp, (z + NZ - 1) % NZ))
    sends.append(lambda: take(red, zn_s))
    take(znext, zn_r)
    pair = z // 2
    zrecv[pair] = red[...] + znext[...]
    for d in FAR_Z:
        if d % 2:
            continue
        send(zrecv.at[pair], zrecv.at[pair], z_s, z_r, (dp, (z + d) % NZ))
    others = zrecv.at[pl.ds(0, NZ // 2 - 1)]
    sends.append(lambda: take(others, z_s))
    take(others, z_r)
    window[...] = jnp.sum(zrecv[...], axis=0) * SCALE

    for d in FAR_XY:
        send(window, window, ag_s, ag_r.at[chip], (chip_at(d), z))
    sends.append(lambda: take(rs_send.at[pl.ds(0, CHIPS - 1)], ag_s))
    for dy in range(4):
        yy = (y + dy) % 4
        for dx in range(1 if dy == 0 else 0, 4):
            xx = (x + dx) % 4
            there = ptf.at[
                pl.ds(aligned(8 * xx, 8), 8), pl.ds(aligned(yy * QUART + core * HALF, LANES), HALF)
            ]
            take(there, ag_r.at[4 * yy + xx])
        block = ptf.at[:, pl.ds(aligned(yy * QUART + core * HALF, LANES), HALF)]
        send(block, block, fwd_s, fwd_r, (sibling, z))
    sends.append(lambda: take(core_recv, fwd_s))
    take(core_recv, fwd_r)

    p_hi, p_lo = split(ptf[...])
    p2 = jnp.concatenate([p_hi, p_lo], axis=0)
    w = dot(grad[...], jnp.concatenate([p2, p2], axis=0), NT)
    wrecv[z] = pack(sum_terms(w))
    for d in FAR_Z:
        send(wrecv.at[z], wrecv.at[z], w_s, w_r, (dp, (z + d) % NZ))
    sends.append(lambda: take(wrecv.at[pl.ds(0, NZ - 1)], w_s))

    part = dot(p2, err[...], NN)
    s_err = part[:R] + part[R:]
    gram = dot(p2, p2, NT)
    gram = gram[:R, :R] + gram[R:, R:] + (gram[:R, R:] + gram[R:, :R])

    linv[...] = inverse_factor(gram)
    first = aligned((3 * z) // 2 * LANES, LANES)
    near = ptf[:, pl.ds(first, 2 * LANES)]
    near = jnp.where(z % 2 == 1, near[:, 64:], near[:, :192])
    basis_ref[...] = jnp.dot(linv[...], near, precision=HIGH, preferred_element_type=F32) * (
        float(D) ** 0.5
    )

    take(wrecv.at[pl.ds(0, NZ - 1)], w_r)
    w_hi, w_lo = split(unpack(wrecv[...].reshape(TOK // 4, LANES)))
    part = dot(jnp.concatenate([w_hi, w_lo], axis=0), hidp[...], NN)
    s_buf[...] = s_err + part[:R] + part[R:]

    my_cols = pl.ds(aligned(core * HALF, LANES), HALF)
    their_cols = pl.ds(aligned((1 - core) * HALF, LANES), HALF)
    send(s_buf.at[:, their_cols], s_core, sc_s, sc_r, (sibling, z))
    sends.append(lambda: take(s_core, sc_s))
    take(s_core, sc_r)
    mine = s_buf[:, my_cols] + s_core[...]

    def exchange(along_x, along_y, sx_s, sx_r, sy_s, sy_r):
        for d in range(1, 4):
            to = 2 * (4 * y + (x + d) % 4) + core
            send(along_x.at[x], along_x.at[x], sx_s, sx_r, (to, z))
            to = 2 * (4 * ((y + d) % 4) + x) + core
            send(along_y.at[y], along_y.at[y], sy_s, sy_r, (to, z))
        sends.append(lambda: take(along_x.at[pl.ds(0, 3)], sx_s))
        sends.append(lambda: take(along_y.at[pl.ds(0, 3)], sy_s))

    sx[x] = mine[: R // 2]
    sy[y] = mine[R // 2 :]
    exchange(sx, sy, sx_s, sx_r, sy_s, sy_r)

    take(sx.at[pl.ds(0, 3)], sx_r)
    take(sy.at[pl.ds(0, 3)], sy_r)
    sy2[y] = jnp.sum(sx[...], axis=0)
    sx2[x] = jnp.sum(sy[...], axis=0)
    exchange(sx2, sy2, sx2_s, sx2_r, sy2_s, sy2_r)
    take(sx2.at[pl.ds(0, 3)], sx2_r)
    take(sy2.at[pl.ds(0, 3)], sy2_r)
    s = jnp.concatenate([jnp.sum(sy2[...], axis=0), jnp.sum(sx2[...], axis=0)], axis=0)
    my_q = qnew_ref.at[:, my_cols]
    my_q[...] = jnp.dot(linv[...], s, precision=HIGH, preferred_element_type=F32) * (1.0 / DP)
    send(my_q, my_q, q_s, q_r, (sibling, z))
    sends.append(lambda: take(s_core, q_s))
    take(qnew_ref.at[:, their_cols], q_r)
    finish()


def body(grad_out, hidden, error, q_init):
    one, many = pltpu.SemaphoreType.DMA, lambda n: pltpu.SemaphoreType.DMA((n,))
    vmem = pltpu.VMEM
    basis, q_new = pl.pallas_call(
        kernel,
        out_shape=(
            jax.ShapeDtypeStruct((R, D // NZ), F32),
            jax.ShapeDtypeStruct((R, F), F32),
        ),
        in_specs=[pl.BlockSpec(memory_space=pltpu.HBM)] * 4,
        out_specs=[pl.BlockSpec(memory_space=pltpu.VMEM)] * 2,
        scratch_shapes=[
            vmem((TOK // NZ, D), BF16),
            vmem((TOK, F), BF16),
            vmem((D, F), BF16),
            vmem((R, F), F32),
            vmem((TOK, F), BF16),
            vmem((R, D), F32),
            vmem((NZ, 4, LANES), F32),
            vmem((NZ - 1, 4, LANES), F32),
            vmem((4, R, HALF), F32),
            vmem((CHIPS, 8, HALF), F32),
            vmem((CHIPS, 8, HALF), F32),
            vmem((8, HALF), F32),
            vmem((8, HALF), F32),
            vmem((NZ // 2, 8, HALF), F32),
            vmem((R, D), F32),
            vmem((NZ, 4, LANES), F32),
            vmem((R, F), F32),
            vmem((R, HALF), F32),
            vmem((4, R // 2, HALF), F32),
            vmem((4, R // 2, HALF), F32),
            vmem((4, R // 2, HALF), F32),
            vmem((4, R // 2, HALF), F32),
            vmem((R, R), F32),
            many(7),
            one, one,
            one, many(4),
            one, one,
            one, one,
            one, one,
            one, many(CHIPS),
            one, one,
            one, one,
            one, one,
            one, one,
            one, one,
            one, one,
            one, one,
            one, one,
        ],
        compiler_params=pltpu.CompilerParams(
            collective_id=0, has_side_effects=True, vmem_limit_bytes=60 * 1024 * 1024
        ),
    )(grad_out[0], hidden[0], error[0], q_init.T)
    return basis.T, q_new.T


def solution(mesh):
    return jax.shard_map(
        body,
        mesh=mesh,
        in_specs=(
            P("dp", "tensor", None),
            P("dp", None, "tensor"),
            P("dp", None, "tensor"),
            P("tensor", None),
        ),
        out_specs=(P("tensor", None), P("tensor", None)),
        check_vma=False,
    )
```

time: 79.6 us -> 68.9 us (0.87)
  Pallas kernels: 75.8 us -> 65.2 us
    pallas_call x1, Pallas kernels: 75.8 us -> 65.2 us  [body(): pl.pallas_call(kernel, out_shape=(jax.ShapeDtypeStruct((R, D // NZ), F32)...]
where the time goes in v2:
time: 68.9 us; the launch traced here: 68.7 us
  Pallas kernels  65.2 us (95%)
  local copies, waits for them, and re-layouts  2.91 us (4%)
    pallas_call x1, Pallas kernels, body(): pl.pallas_call(kernel, out_shape=(jax.ShapeDtypeStruct((R, D // NZ), F32)...  65.2 us
    unnamed x2, local copies, waits for them, and re-layouts  2.91 us

profile of v2, /device:TPU:1, one launch (start us, length us, event | category | flops | bytes accessed | tf_op | source)
XLA Modules:
  0.0 68.7 jit_solution(11419068674437149305)
XLA Ops:
  0.6 65.2 %shard_map.59 = (f32[32,192]{1,0:T(8,128)}, f32[32,768]{1,0:T(8,128)}) custom-call(bf16[16,3072]{1,0:T(8,128)(2,1)} %bitcast.9, bf16[256,768]{1,0:T(8,128)(2,1)} %bitcast.7, bf16[3072,768]{1,0:T(8,128)(2,1)} %bitcast.6, f32[32,768]{1,0:T(8,128)} %bitcast.10), custom_call_target="tpu_custom_call" | custom-call | tf_op jit(solution)/shard_map/pallas_call | solution.py:269
  65.8 1.4 %copy.8 = f32[192,32]{0,1:T(8,128)} copy(f32[192,32]{0,1:T(8,128)} %bitcast.11) | data formatting | bytes 49152
  67.2 1.5 %copy.9 = f32[768,32]{0,1:T(8,128)} copy(f32[768,32]{0,1:T(8,128)} %bitcast.8) | data formatting | bytes 196608

commit v3 on v2

--- a/solution.py
+++ b/solution.py
@@ -16,6 +16,7 @@
 NZ, CHIPS, DP = 16, 16, 32
 D, F, R, TOK = 3072, 768, 32, 256
 LANES, HALF, QUART = 128, 384, 768
+FAR = (2, 1, 3, 0)
 FAR_Z = sorted(range(1, NZ), key=lambda d: -min(d, NZ - d))
 FAR_XY = sorted(range(1, CHIPS), key=lambda d: -min(d % 4, 4 - d % 4) - min(d // 4, 4 - d // 4))
 SCALE = 2.0**20
@@ -70,8 +71,8 @@
 def kernel(
     grad_hbm, hid_hbm, err_hbm, qt_hbm, basis_ref, qnew_ref,
     grad, hid, err, qt, hidp, pt, img_send, img_recv, core_recv, rs_send, rs_recv,
-    red, znext, zrecv, ptf, wrecv, s_buf, s_core, sx, sy, sx2, sy2, linv,
-    loc, img_s, img_r, core_s, core_r, rs_s, rs_r, zn_s, zn_r, z_s, z_r,
+    zrecv, ptf, wrecv, s_buf, s_core, sx, sy, sx2, sy2, linv,
+    loc, img_s, img_r, core_s, core_r, rs_s, rs_r, z_s, z_r,
     ag_s, ag_r, fwd_s, fwd_r, w_s, w_r, sc_s, sc_r, sx_s, sx_r, sy_s, sy_r,
     sx2_s, sx2_r, sy2_s, sy2_r, q_s, q_r,
 ):
@@ -80,6 +81,8 @@
     core, chip = dp % 2, dp // 2
     x, y = chip % 4, chip // 4
     sibling = dp + 1 - 2 * core
+    odd, pair = z % 2, z // 2
+    partner = z + 1 - 2 * odd
 
     def chip_at(d):
         return 2 * (4 * ((y + d // 4) % 4) + (x + d % 4) % 4) + core
@@ -110,6 +113,7 @@
     for d in FAR_XY:
         to = chip_at(d)
         pl.semaphore_signal(barrier, 1, device_id=(to, z), device_id_type=MESH)
+        pl.semaphore_signal(barrier, 1, device_id=(to, partner), device_id_type=MESH)
     for d in FAR_Z:
         pl.semaphore_signal(barrier, 1, device_id=(dp, (z + d) % NZ), device_id_type=MESH)
 
@@ -127,7 +131,7 @@
     images = sum_terms(dot(hid[...], jnp.concatenate([q2, q2], axis=0), NT))
     img_send[...] = pack(images.reshape(NZ, BLOCK, LANES))
     loads[2].wait()
-    pl.semaphore_wait(barrier, CHIPS + NZ - 1)
+    pl.semaphore_wait(barrier, 2 * CHIPS + NZ - 2)
     for d in FAR_Z:
         to = (z + d) % NZ
         send(img_send.at[to], img_recv.at[d - 1], img_s, img_r, (dp, to))
@@ -144,38 +148,34 @@
     take(img_recv, img_r)
     im_hi, im_lo = split(unpack(jnp.sum(img_recv[...], axis=0) + img_send[z]))
     im2 = jnp.concatenate([im_hi, im_lo], axis=0)
-    for c in range(4):
-        cols = pl.ds(c * QUART, QUART)
+    for dy in FAR:
+        c = (y + dy) % 4
+        cols = pl.ds(aligned(c * QUART, LANES), QUART)
         part = dot(im2, grad[:, cols], NN)
         pt[:, cols] += part[:R] + part[R:]
         theirs = pl.ds(aligned(c * QUART + (1 - core) * HALF, LANES), HALF)
         send(pt.at[:, theirs], core_recv.at[c], core_s, core_r.at[c], (sibling, z))
     sends.append(lambda: take(core_recv, core_s))
 
-    for c in range(4):
+    for dy in FAR:
+        c = (y + dy) % 4
         take(core_recv.at[c], core_r.at[c])
         mine = pt[:, pl.ds(aligned(c * QUART + core * HALF, LANES), HALF)] + core_recv[c]
         for g in range(4):
-            t = 4 * c + g
-            rs_send[t] = mine[8 * g : 8 * g + 8]
-
-            @pl.when(t != chip)
-            def _(t=t):
-                send(rs_send.at[t], rs_recv.at[chip], rs_s, rs_r, (2 * t + core, z))
-
-    sends.append(lambda: take(rs_send.at[pl.ds(0, CHIPS - 1)], rs_s))
-    rs_recv[chip] = rs_send[chip]
-    take(rs_recv.at[pl.ds(0, CHIPS - 1)], rs_r)
-    red[...] = jnp.sum(rs_recv[...], axis=0)
-
-    rows = pl.ds(aligned(8 * x, 8), 8)
-    base = y * QUART + core * HALF
-    window = ptf.at[rows, pl.ds(aligned(base, LANES), HALF)]
-    send(red, znext, zn_s, zn_r, (dp, (z + NZ - 1) % NZ))
-    sends.append(lambda: take(red, zn_s))
-    take(znext, zn_r)
-    pair = z // 2
-    zrecv[pair] = red[...] + znext[...]
+            rs_send[4 * c + g] = mine[8 * g : 8 * g + 8]
+        for dx in FAR:
+            t = 4 * c + (x + dx) % 4
+            for to, first in ((partner, 1 - odd), (z, odd)):
+                if dy or dx or to is partner:
+                    src = rs_send.at[t, :, pl.ds(aligned(first * LANES, LANES), 2 * LANES)]
+                    send(src, rs_recv.at[2 * chip + odd], rs_s, rs_r, (2 * t + core, to))
+    heard = rs_recv.at[pl.ds(0, 2 * CHIPS - 1)]
+    sends.append(lambda: take(heard, rs_s))
+    mine = pl.ds(aligned(odd * LANES, LANES), 2 * LANES)
+    rs_recv[2 * chip + odd] = rs_send[chip, :, mine]
+    take(heard, rs_r)
+
+    zrecv[pair] = jnp.sum(rs_recv[...], axis=0)
     for d in FAR_Z:
         if d % 2:
             continue
@@ -183,11 +183,40 @@
     others = zrecv.at[pl.ds(0, NZ // 2 - 1)]
     sends.append(lambda: take(others, z_s))
     take(others, z_r)
-    window[...] = jnp.sum(zrecv[...], axis=0) * SCALE
-
-    for d in FAR_XY:
-        send(window, window, ag_s, ag_r.at[chip], (chip_at(d), z))
-    sends.append(lambda: take(rs_send.at[pl.ds(0, CHIPS - 1)], ag_s))
+    rows = pl.ds(aligned(8 * x, 8), 8)
+    base = y * QUART + core * HALF
+    sums = jnp.sum(zrecv[...], axis=0) * SCALE
+    first_two = ptf.at[rows, pl.ds(aligned(base, LANES), 2 * LANES)]
+    last = ptf.at[rows, pl.ds(aligned(base + 2 * LANES, LANES), LANES)]
+
+    def spread(window):
+        for d in FAR_XY:
+            send(window, window, ag_s, ag_r.at[chip], (chip_at(d), partner))
+            send(window, window, ag_s, ag_r.at[chip], (chip_at(d), z))
+        send(window, window, ag_s, ag_r.at[chip], (dp, partner))
+
+    @pl.when(odd == 0)
+    def _():
+        first_two[...] = sums
+        spread(first_two)
+        take(last, ag_r.at[chip])
+
+    @pl.when(odd == 1)
+    def _():
+        last[...] = sums[:, LANES:]
+        spread(last)
+        take(first_two, ag_r.at[chip])
+
+    def spread_sends():
+        @pl.when(odd == 0)
+        def _():
+            take(heard, ag_s)
+
+        @pl.when(odd == 1)
+        def _():
+            take(rs_recv.at[pl.ds(0, 2 * CHIPS - 1), :, pl.ds(0, LANES)], ag_s)
+
+    sends.append(spread_sends)
     for dy in range(4):
         yy = (y + dy) % 4
         for dx in range(1 if dy == 0 else 0, 4):
@@ -207,7 +236,8 @@
     wrecv[z] = pack(sum_terms(w))
     for d in FAR_Z:
         send(wrecv.at[z], wrecv.at[z], w_s, w_r, (dp, (z + d) % NZ))
-    sends.append(lambda: take(wrecv.at[pl.ds(0, NZ - 1)], w_s))
+    far = wrecv.at[pl.ds(0, NZ - 1)]
+    sends.append(lambda: take(far, w_s))
 
     part = dot(p2, err[...], NN)
     s_err = part[:R] + part[R:]
@@ -216,13 +246,13 @@
 
     linv[...] = inverse_factor(gram)
     first = aligned((3 * z) // 2 * LANES, LANES)
-    near = ptf[:, pl.ds(first, 2 * LANES)]
-    near = jnp.where(z % 2 == 1, near[:, 64:], near[:, :192])
-    basis_ref[...] = jnp.dot(linv[...], near, precision=HIGH, preferred_element_type=F32) * (
+    mid = ptf[:, pl.ds(first, 2 * LANES)]
+    mid = jnp.where(z % 2 == 1, mid[:, 64:], mid[:, :192])
+    basis_ref[...] = jnp.dot(linv[...], mid, precision=HIGH, preferred_element_type=F32) * (
         float(D) ** 0.5
     )
 
-    take(wrecv.at[pl.ds(0, NZ - 1)], w_r)
+    take(far, w_r)
     w_hi, w_lo = split(unpack(wrecv[...].reshape(TOK // 4, LANES)))
     part = dot(jnp.concatenate([w_hi, w_lo], axis=0), hidp[...], NN)
     s_buf[...] = s_err + part[:R] + part[R:]
@@ -268,14 +298,11 @@
     vmem = pltpu.VMEM
     basis, q_new = pl.pallas_call(
         kernel,
-        out_shape=(
-            jax.ShapeDtypeStruct((R, D // NZ), F32),
-            jax.ShapeDtypeStruct((R, F), F32),
-        ),
+        out_shape=(pltpu.VMEM((R, D // NZ), F32), pltpu.VMEM((R, F), F32)),
         in_specs=[pl.BlockSpec(memory_space=pltpu.HBM)] * 4,
         out_specs=[pl.BlockSpec(memory_space=pltpu.VMEM)] * 2,
         scratch_shapes=[
-            vmem((TOK // NZ, D), BF16),
+            vmem((BLOCK, D), BF16),
             vmem((TOK, F), BF16),
             vmem((D, F), BF16),
             vmem((R, F), F32),
@@ -285,10 +312,8 @@
             vmem((NZ - 1, 4, LANES), F32),
             vmem((4, R, HALF), F32),
             vmem((CHIPS, 8, HALF), F32),
-            vmem((CHIPS, 8, HALF), F32),
-            vmem((8, HALF), F32),
-            vmem((8, HALF), F32),
-            vmem((NZ // 2, 8, HALF), F32),
+            vmem((2 * CHIPS, 8, 2 * LANES), F32),
+            vmem((NZ // 2, 8, 2 * LANES), F32),
             vmem((R, D), F32),
             vmem((NZ, 4, LANES), F32),
             vmem((R, F), F32),
@@ -301,7 +326,6 @@
             many(7),
             one, one,
             one, many(4),
-            one, one,
             one, one,
             one, one,
             one, many(CHIPS),

time: 68.9 us -> 64.2 us (0.932)
  Pallas kernels: 65.2 us -> 62.2 us
  local copies, waits for them, and re-layouts: 2.91 us -> 1.26 us
    pallas_call x1, Pallas kernels: 65.2 us -> 62.2 us  [body(): pl.pallas_call(kernel, out_shape=(pltpu.VMEM((R, D // NZ), F32), pltpu.VM...]
    unnamed x2, local copies, waits for them, and re-layouts: 2.91 us -> 1.26 us
where the time goes in v3:
time: 64.2 us; the launch traced here: 64.1 us
  Pallas kernels  62.2 us (97%)
  local copies, waits for them, and re-layouts  1.26 us (2%)
    pallas_call x1, Pallas kernels, body(): pl.pallas_call(kernel, out_shape=(pltpu.VMEM((R, D // NZ), F32), pltpu.VM...  62.2 us

profile of v3, /device:TPU:1, one launch (start us, length us, event | category | flops | bytes accessed | tf_op | source)
XLA Modules:
  0.0 64.1 jit_solution(12538451380267610597)
XLA Ops:
  0.6 62.2 %shard_map.59 = (f32[32,192]{1,0:T(8,128)S(1)}, f32[32,768]{1,0:T(8,128)S(1)}) custom-call(bf16[16,3072]{1,0:T(8,128)(2,1)} %bitcast.10, bf16[256,768]{1,0:T(8,128)(2,1)} %bitcast.9, bf16[3072,768]{1,0:T(8,128)(2,1)} %bitcast.8, f32[32,768]{1,0:T(8,128)} %bitcast.11), custom_call_target="tpu_custom_call" | custom-call | tf_op jit(solution)/shard_map/pallas_call | solution.py:299
  62.8 0.6 copy.8
  63.4 0.6 copy.9

commit v4 on v3

--- a/solution.py
+++ b/solution.py
@@ -74,7 +74,7 @@
     zrecv, ptf, wrecv, s_buf, s_core, sx, sy, sx2, sy2, linv,
     loc, img_s, img_r, core_s, core_r, rs_s, rs_r, z_s, z_r,
     ag_s, ag_r, fwd_s, fwd_r, w_s, w_r, sc_s, sc_r, sx_s, sx_r, sy_s, sy_r,
-    sx2_s, sx2_r, sy2_s, sy2_r, q_s, q_r,
+    sx2_s, sx2_r, sy2_s, sy2_r,
 ):
     dp = lax.axis_index("dp")
     z = lax.axis_index("tensor")
@@ -93,6 +93,19 @@
             device_id=to, device_id_type=MESH,
         )
         copy.start()
+
+    barrier = pltpu.get_barrier_semaphore()
+    for d in FAR_Z:
+        pl.semaphore_signal(barrier, 1, device_id=(dp, (z + d) % NZ), device_id_type=MESH)
+    pl.semaphore_signal(barrier, 1, device_id=(sibling, z), device_id_type=MESH)
+    for d in FAR[:3]:
+        for to in (chip_at(d), chip_at(4 * d)):
+            to = to + 1 - 2 * core
+            pl.semaphore_signal(barrier, 1, device_id=(to, z), device_id_type=MESH)
+    for d in FAR_XY:
+        to = chip_at(d)
+        pl.semaphore_signal(barrier, 1, device_id=(to, z), device_id_type=MESH)
+        pl.semaphore_signal(barrier, 1, device_id=(to, partner), device_id_type=MESH)
 
     loads = [
         pltpu.make_async_copy(qt_hbm, qt, loc.at[0]),
@@ -108,15 +121,6 @@
     for load in loads:
         load.start()
 
-    barrier = pltpu.get_barrier_semaphore()
-    pl.semaphore_signal(barrier, 1, device_id=(sibling, z), device_id_type=MESH)
-    for d in FAR_XY:
-        to = chip_at(d)
-        pl.semaphore_signal(barrier, 1, device_id=(to, z), device_id_type=MESH)
-        pl.semaphore_signal(barrier, 1, device_id=(to, partner), device_id_type=MESH)
-    for d in FAR_Z:
-        pl.semaphore_signal(barrier, 1, device_id=(dp, (z + d) % NZ), device_id_type=MESH)
-
     sends = []
 
     def finish():
@@ -131,7 +135,7 @@
     images = sum_terms(dot(hid[...], jnp.concatenate([q2, q2], axis=0), NT))
     img_send[...] = pack(images.reshape(NZ, BLOCK, LANES))
     loads[2].wait()
-    pl.semaphore_wait(barrier, 2 * CHIPS + NZ - 2)
+    pl.semaphore_wait(barrier, 2 * CHIPS + NZ + 4)
     for d in FAR_Z:
         to = (z + d) % NZ
         send(img_send.at[to], img_recv.at[d - 1], img_s, img_r, (dp, to))
@@ -264,32 +268,40 @@
     take(s_core, sc_r)
     mine = s_buf[:, my_cols] + s_core[...]
 
-    def exchange(along_x, along_y, sx_s, sx_r, sy_s, sy_r):
-        for d in range(1, 4):
-            to = 2 * (4 * y + (x + d) % 4) + core
-            send(along_x.at[x], along_x.at[x], sx_s, sx_r, (to, z))
-            to = 2 * (4 * ((y + d) % 4) + x) + core
-            send(along_y.at[y], along_y.at[y], sy_s, sy_r, (to, z))
-        sends.append(lambda: take(along_x.at[pl.ds(0, 3)], sx_s))
-        sends.append(lambda: take(along_y.at[pl.ds(0, 3)], sy_s))
+    def exchange(along_x, at_x, along_y, at_y, sems, both):
+        sx_s, sx_r, sy_s, sy_r = sems
+        x_block, y_block = along_x.at[at_x], along_y.at[at_y]
+        for d in FAR if both else FAR[:3]:
+            for to, block, s, r in (
+                (chip_at(d), x_block, sx_s, sx_r),
+                (chip_at(4 * d), y_block, sy_s, sy_r),
+            ):
+                if d:
+                    send(block, block, s, r, (to, z))
+                if both:
+                    send(block, block, s, r, (to + 1 - 2 * core, z))
+        n = 7 if both else 3
+        sends.append(lambda: take(along_x.at[pl.ds(0, n)], sx_s))
+        sends.append(lambda: take(along_y.at[pl.ds(0, n)], sy_s))
 
     sx[x] = mine[: R // 2]
     sy[y] = mine[R // 2 :]
-    exchange(sx, sy, sx_s, sx_r, sy_s, sy_r)
+    exchange(sx, x, sy, y, (sx_s, sx_r, sy_s, sy_r), False)
 
     take(sx.at[pl.ds(0, 3)], sx_r)
     take(sy.at[pl.ds(0, 3)], sy_r)
-    sy2[y] = jnp.sum(sx[...], axis=0)
-    sx2[x] = jnp.sum(sy[...], axis=0)
-    exchange(sx2, sy2, sx2_s, sx2_r, sy2_s, sy2_r)
-    take(sx2.at[pl.ds(0, 3)], sx2_r)
-    take(sy2.at[pl.ds(0, 3)], sy2_r)
-    s = jnp.concatenate([jnp.sum(sy2[...], axis=0), jnp.sum(sx2[...], axis=0)], axis=0)
-    my_q = qnew_ref.at[:, my_cols]
-    my_q[...] = jnp.dot(linv[...], s, precision=HIGH, preferred_element_type=F32) * (1.0 / DP)
-    send(my_q, my_q, q_s, q_r, (sibling, z))
-    sends.append(lambda: take(s_core, q_s))
-    take(qnew_ref.at[:, their_cols], q_r)
+    at_x, at_y = 4 * core + x, 4 * core + y
+    sy2[at_y] = jnp.sum(sx[...], axis=0)
+    sx2[at_x] = jnp.sum(sy[...], axis=0)
+    exchange(sx2, at_x, sy2, at_y, (sx2_s, sx2_r, sy2_s, sy2_r), True)
+    take(sx2.at[pl.ds(0, 7)], sx2_r)
+    take(sy2.at[pl.ds(0, 7)], sy2_r)
+    for half in range(2):
+        part = [jnp.sum(v[4 * half : 4 * half + 4], axis=0) for v in (sy2, sx2)]
+        part = jnp.dot(
+            linv[...], jnp.concatenate(part, axis=0), precision=HIGH, preferred_element_type=F32
+        )
+        qnew_ref[:, half * HALF : (half + 1) * HALF] = part * (1.0 / DP)
     finish()
 
 
@@ -320,8 +332,8 @@
             vmem((R, HALF), F32),
             vmem((4, R // 2, HALF), F32),
             vmem((4, R // 2, HALF), F32),
-            vmem((4, R // 2, HALF), F32),
-            vmem((4, R // 2, HALF), F32),
+            vmem((8, R // 2, HALF), F32),
+            vmem((8, R // 2, HALF), F32),
             vmem((R, R), F32),
             many(7),
             one, one,
@@ -329,7 +341,6 @@
             one, one,
             one, one,
             one, many(CHIPS),
-            one, one,
             one, one,
             one, one,
             one, one,

time: 64.2 us -> 63 us (0.981)
  Pallas kernels: 62.2 us -> 60.9 us
    pallas_call x1, Pallas kernels: 62.2 us -> 60.9 us  [body(): pl.pallas_call(kernel, out_shape=(pltpu.VMEM((R, D // NZ), F32), pltpu.VM...]
where the time goes in v4:
time: 63 us; the launch traced here: 62.8 us
  Pallas kernels  60.9 us (97%)
  local copies, waits for them, and re-layouts  1.26 us (2%)
  between operations  0.64 us (1%)
    pallas_call x1, Pallas kernels, body(): pl.pallas_call(kernel, out_shape=(pltpu.VMEM((R, D // NZ), F32), pltpu.VM...  60.9 us

profile of v4, /device:TPU:1, one launch (start us, length us, event | category | flops | bytes accessed | tf_op | source)
XLA Modules:
  0.0 62.8 jit_solution(5283916780409705998)
XLA Ops:
  0.6 60.9 %shard_map.59 = (f32[32,192]{1,0:T(8,128)S(1)}, f32[32,768]{1,0:T(8,128)S(1)}) custom-call(bf16[16,3072]{1,0:T(8,128)(2,1)} %bitcast.10, bf16[256,768]{1,0:T(8,128)(2,1)} %bitcast.9, bf16[3072,768]{1,0:T(8,128)(2,1)} %bitcast.8, f32[32,768]{1,0:T(8,128)} %bitcast.11), custom_call_target="tpu_custom_call" | custom-call | tf_op jit(solution)/shard_map/pallas_call | solution.py:311
  61.6 0.6 copy.8
  62.2 0.6 %copy.9 = f32[768,32]{0,1:T(8,128)} copy(f32[768,32]{0,1:T(8,128)S(1)} %bitcast.6) | data formatting | bytes 196608

commit v5 on v4

--- a/solution.py
+++ b/solution.py
@@ -126,6 +126,7 @@
     def finish():
         for fn in sends:
             fn()
+        sends.clear()
 
 
     loads[0].wait()
@@ -221,16 +222,14 @@
             take(rs_recv.at[pl.ds(0, 2 * CHIPS - 1), :, pl.ds(0, LANES)], ag_s)
 
     sends.append(spread_sends)
-    for dy in range(4):
-        yy = (y + dy) % 4
-        for dx in range(1 if dy == 0 else 0, 4):
-            xx = (x + dx) % 4
-            there = ptf.at[
-                pl.ds(aligned(8 * xx, 8), 8), pl.ds(aligned(yy * QUART + core * HALF, LANES), HALF)
-            ]
+    for d in [0] + FAR_XY[::-1]:
+        yy, xx = (y + d // 4) % 4, (x + d % 4) % 4
+        there = ptf.at[
+            pl.ds(aligned(8 * xx, 8), 8), pl.ds(aligned(yy * QUART + core * HALF, LANES), HALF)
+        ]
+        if d:
             take(there, ag_r.at[4 * yy + xx])
-        block = ptf.at[:, pl.ds(aligned(yy * QUART + core * HALF, LANES), HALF)]
-        send(block, block, fwd_s, fwd_r, (sibling, z))
+        send(there, there, fwd_s, fwd_r, (sibling, z))
     sends.append(lambda: take(core_recv, fwd_s))
     take(core_recv, fwd_r)
 
@@ -240,11 +239,12 @@
     wrecv[z] = pack(sum_terms(w))
     for d in FAR_Z:
         send(wrecv.at[z], wrecv.at[z], w_s, w_r, (dp, (z + d) % NZ))
+    finish()
     far = wrecv.at[pl.ds(0, NZ - 1)]
     sends.append(lambda: take(far, w_s))
 
     part = dot(p2, err[...], NN)
-    s_err = part[:R] + part[R:]
+    s_buf[...] = part[:R] + part[R:]
     gram = dot(p2, p2, NT)
     gram = gram[:R, :R] + gram[R:, R:] + (gram[:R, R:] + gram[R:, :R])
 
@@ -258,12 +258,15 @@
 
     take(far, w_r)
     w_hi, w_lo = split(unpack(wrecv[...].reshape(TOK // 4, LANES)))
-    part = dot(jnp.concatenate([w_hi, w_lo], axis=0), hidp[...], NN)
-    s_buf[...] = s_err + part[:R] + part[R:]
+    w2 = jnp.concatenate([w_hi, w_lo], axis=0)
 
     my_cols = pl.ds(aligned(core * HALF, LANES), HALF)
     their_cols = pl.ds(aligned((1 - core) * HALF, LANES), HALF)
+    part = dot(w2, hidp[:, their_cols], NN)
+    s_buf[:, their_cols] += part[:R] + part[R:]
     send(s_buf.at[:, their_cols], s_core, sc_s, sc_r, (sibling, z))
+    part = dot(w2, hidp[:, my_cols], NN)
+    s_buf[:, my_cols] += part[:R] + part[R:]
     sends.append(lambda: take(s_core, sc_s))
     take(s_core, sc_r)
     mine = s_buf[:, my_cols] + s_core[...]
@@ -293,7 +296,10 @@
     at_x, at_y = 4 * core + x, 4 * core + y
     sy2[at_y] = jnp.sum(sx[...], axis=0)
     sx2[at_x] = jnp.sum(sy[...], axis=0)
+    early, sends[:] = list(sends), []
     exchange(sx2, at_x, sy2, at_y, (sx2_s, sx2_r, sy2_s, sy2_r), True)
+    for fn in early:
+        fn()
     take(sx2.at[pl.ds(0, 7)], sx2_r)
     take(sy2.at[pl.ds(0, 7)], sy2_r)
     for half in range(2):

time: 63 us -> 62.8 us (level)
  no operation moved by 1% of the time
where the time goes in v5:
time: 62.8 us; the launch traced here: 62.7 us
  Pallas kernels  60.8 us (97%)
  local copies, waits for them, and re-layouts  1.26 us (2%)
  between operations  0.64 us (1%)
    pallas_call x1, Pallas kernels, body(): pl.pallas_call(kernel, out_shape=(pltpu.VMEM((R, D // NZ), F32), pltpu.VM...  60.8 us
    unnamed x2, local copies, waits for them, and re-layouts  1.26 us

profile of v5, /device:TPU:1, one launch (start us, length us, event | category | flops | bytes accessed | tf_op | source)
XLA Modules:
  0.0 62.7 jit_solution(14253520107597908822)
XLA Ops:
  0.6 60.8 %shard_map.59 = (f32[32,192]{1,0:T(8,128)S(1)}, f32[32,768]{1,0:T(8,128)S(1)}) custom-call(bf16[16,3072]{1,0:T(8,128)(2,1)} %bitcast.10, bf16[256,768]{1,0:T(8,128)(2,1)} %bitcast.9, bf16[3072,768]{1,0:T(8,128)(2,1)} %bitcast.8, f32[32,768]{1,0:T(8,128)} %bitcast.11), custom_call_target="tpu_custom_call" | custom-call | tf_op jit(solution)/shard_map/pallas_call | solution.py:317
  61.4 0.6 copy.8
  62.1 0.6 %copy.9 = f32[768,32]{0,1:T(8,128)} copy(f32[768,32]{0,1:T(8,128)S(1)} %bitcast.6) | data formatting | bytes 196608
